TPU v7x, 32 devices: a whole 2x2x4 slice. The times are simulated.
32 devices in a mesh: groups: 2 (over y), win: 4 (over z), head: 2 (over x), sub: 2 (over core).
Axes of the slice: x: 2, y: 2, z: 4, core: 2. Of those that a mesh axis runs over, the one named last changes fastest.
Arguments:
- queries: float32 [2048, 6144], P(('groups', 'win'), ('head', 'sub')), parts along dimension 0, may hold values from -6.5 to 6.5
- key_rows: float32 [2048, 6144], P(('groups', 'win'), ('head', 'sub')), parts along dimension 0, may hold values from -6.5 to 6.5
- value_rows: float32 [2048, 6144], P(('groups', 'win'), ('head', 'sub')), parts along dimension 0, may hold values from -6 to 6
- merge_target: int32 [2048], P(('groups', 'win')), parts along dimension 0, may hold values from 0 to 831, as said below
Outputs:
- attended: float32 [2048, 6144], P(('groups', 'win'), ('head', 'sub')), parts along dimension 0
There are 2 independent parts, one for each index of `groups`. A program takes and returns all parts, laid end to end along the dimension named above; each array names one. Nothing has to cross between parts.
Inputs may be any that keep to these rules, and one draw needn't show every extreme that they name: merge_target[r] lies in window merge_target[r] // 208; every merged row is joined by one or more rows; of the rows of one window, at most 64 join merged rows of any one window, exactly 64 join those of some window, and at least 52 join those of every window.
All inputs are finite; a program needn't handle non-finite values.
Results may differ from a plain program's by a relative error of at most 0.0003.
Values sent between devices are 32-bit elements; how exact they have to be, the bound alone decides.
A program may use at most 64 MiB of HBM per device.

v0:
```python
import math

import jax
import jax.numpy as jnp
from jax import lax
from jax.sharding import PartitionSpec as P

HEAD_DIM = 128
ROWS_PER_WINDOW = 256
MERGED_WINDOW_ROWS = 208


def slot_layout(merge_target, window_count, capacity):
    target_window = merge_target // MERGED_WINDOW_ROWS
    target_place = merge_target % MERGED_WINDOW_ROWS
    member = (target_window[:, None] == jnp.arange(window_count, dtype=jnp.int32)[None, :]).astype(
        jnp.int32
    )
    earlier = jnp.cumsum(member, axis=0) - member
    position = jnp.sum(earlier * member, axis=1)
    slot_index = target_window * capacity + position
    slot_total = window_count * capacity
    row_count = merge_target.shape[0]
    source_row = (
        jnp.full((slot_total,), row_count, jnp.int32)
        .at[slot_index]
        .set(jnp.arange(row_count, dtype=jnp.int32))
    )
    labels_flat = (
        jnp.zeros((slot_total,), jnp.float32)
        .at[slot_index]
        .set((target_place + 1).astype(jnp.float32))
    )
    return (slot_index, source_row, labels_flat.reshape(window_count, capacity))


def pack_rows(source, source_row, window_count, capacity):
    padding = jnp.zeros((1, source.shape[1]), source.dtype)
    return jnp.concatenate([source, padding], 0)[source_row].reshape(
        window_count, capacity, source.shape[1]
    )


def slot_counts(labels):
    label_index = labels.reshape(-1).astype(jnp.int32) - 1
    segment = jnp.where(label_index < 0, MERGED_WINDOW_ROWS, label_index)
    counts = jax.ops.segment_sum(
        jnp.ones(segment.shape, jnp.float32), segment, MERGED_WINDOW_ROWS + 1
    )[:MERGED_WINDOW_ROWS]
    return (segment, counts)


def average_slots(received, segment, counts):
    flattened = received.reshape(-1, received.shape[-1])
    totals = jax.ops.segment_sum(flattened, segment, MERGED_WINDOW_ROWS + 1)[:MERGED_WINDOW_ROWS]
    return totals / counts[:, None]


def local(queries, key_rows, value_rows, merge_target):
    window_count = lax.axis_size("win")
    capacity = MERGED_WINDOW_ROWS // window_count + (ROWS_PER_WINDOW - MERGED_WINDOW_ROWS) // 4
    col_width = queries.shape[1]
    head_count = col_width // HEAD_DIM
    slot_index, source_row, labels = slot_layout(merge_target, window_count, capacity)
    pair_rows = jnp.concatenate([key_rows, value_rows], 1)
    packed_pair = pack_rows(pair_rows, source_row, window_count, capacity)
    received_pair, got_labels = (
        lax.all_to_all(packed_pair, "win", split_axis=0, concat_axis=0, tiled=True),
        lax.all_to_all(labels, "win", split_axis=0, concat_axis=0, tiled=True),
    )
    segment, counts = slot_counts(got_labels)
    merged_pair = average_slots(received_pair, segment, counts)
    merged_keys = merged_pair[:, :col_width]
    merged_values = merged_pair[:, col_width:]
    packed_queries = pack_rows(queries, source_row, window_count, capacity)
    received_queries = lax.all_to_all(
        packed_queries, "win", split_axis=0, concat_axis=0, tiled=True
    )
    merged_queries = average_slots(received_queries, segment, counts)
    scaling = 1.0 / math.sqrt(HEAD_DIM)
    query_head_stack = merged_queries.reshape(MERGED_WINDOW_ROWS, head_count, HEAD_DIM)
    running_max = jnp.full((head_count, MERGED_WINDOW_ROWS), -1e30, jnp.float32)
    portion_keys = lax.all_gather(merged_keys, "win", axis=0, tiled=True)
    portion_values = lax.all_gather(merged_values, "win", axis=0, tiled=True)
    key_head_stack = portion_keys.reshape(-1, head_count, HEAD_DIM)
    value_head_stack = portion_values.reshape(-1, head_count, HEAD_DIM)
    scores = (
        jnp.einsum(
            "frk,grk->rfg", query_head_stack, key_head_stack, precision=lax.Precision.HIGHEST
        )
        * scaling
    )
    new_max = jnp.maximum(running_max, jnp.max(scores, axis=2))
    attention_weight = jnp.exp(scores - new_max[:, :, None])
    new_sum = jnp.sum(attention_weight, axis=2)
    appended_rows = jnp.einsum(
        "tak,ktl->atl", attention_weight, value_head_stack, precision=lax.Precision.HIGHEST
    )
    merged_output = (appended_rows / jnp.transpose(new_sum)[:, :, None]).reshape(
        MERGED_WINDOW_ROWS, col_width
    )
    padded_output = jnp.concatenate([merged_output, jnp.zeros((1, col_width), jnp.float32)], 0)
    outgoing = padded_output[segment].reshape(window_count, capacity, col_width)
    returned = lax.all_to_all(outgoing, "win", split_axis=0, concat_axis=0, tiled=True)
    return returned.reshape(-1, col_width)[slot_index]


def solution(mesh):
    return jax.shard_map(
        local,
        mesh=mesh,
        in_specs=(
            P(("groups", "win"), ("head", "sub")),
            P(("groups", "win"), ("head", "sub")),
            P(("groups", "win"), ("head", "sub")),
            P(("groups", "win")),
        ),
        out_specs=P(("groups", "win"), ("head", "sub")),
        check_vma=False,
    )
```

profile of v0, /device:TPU:9, one launch (start us, length us, event | category | flops | bytes accessed | tf_op | source)
XLA Modules:
  0.0 399.7 jit_solution(8568793867062111420)
XLA Ops:
  6.5 0.7 fusion.17
  7.2 1.2 reduce-window.6
  8.5 0.1 slice.36
  8.5 0.1 copy.14
  8.7 0.1 copy.15
  8.8 0.1 add_bitcast_fusion
  8.9 1.4 scatter_custom_fusion
  10.3 0.7 all_to_all.15
  11.0 4.8 %all-to-all-start = ((f32[4,1,64]{2,1,0:T(1,128)}), f32[4,1,64]{2,1,0:T(1,128)S(1)}, u32[]{:S(2)}, u32[]{:S(2)}) async-start(f32[4,1,64]{2,1,0:T(1,128)} %all_to_all.15), calls=%async_computation | async-start | bytes 4096 | tf_op jit(solution)/shard_map/all_to_all | solution.py:69
  15.7 1.4 scatter_custom_fusion.1
  17.1 2.2 select_maximum_fusion
  19.4 3.3 gather_fusion
  22.7 0.0 all-to-all-done
  22.7 4.5 %all-to-all-start.1 = ((f32[4,64,3072]{2,1,0:T(8,128)}), f32[4,64,3072]{2,1,0:T(8,128)S(1)}, u32[]{:S(2)}, u32[]{:S(2)}) async-start(f32[4,64,3072]{2,1,0:T(8,128)} %bitcast.55), calls=%async_computation.1 | async-start | bytes 6291456 | tf_op jit(solution)/shard_map/all_to_all | solution.py:68
  27.3 0.0 all-gather.5.cloned.1.call-start
  27.3 0.1 sub.25
  27.4 2.3 scatter_custom_fusion.3
  29.7 63.8 %all-to-all-done.1 = f32[4,64,3072]{2,1,0:T(8,128)S(1)} async-done(((f32[4,64,3072]{2,1,0:T(8,128)}), f32[4,64,3072]{2,1,0:T(8,128)S(1)}, u32[]{:S(2)}, u32[]{:S(2)}) %all-to-all-start.1) | async-done | bytes 3145760 | tf_op jit(solution)/shard_map/all_to_all | solution.py:68
  93.5 0.0 copy-start.1
  93.5 1.7 copy-done.1
  95.1 6.6 %scatter_custom_fusion.2 = f32[209,3072]{1,0:T(8,128)S(1)} fusion(s32[256]{0:T(256)S(1)} %bitcast.66, f32[256,3072]{1,0:T(8,128)} %bitcast.57, f32[]{:T(128)} %constant.14.clone.1), kind=kCustom, calls=%fused_computation.19 | custom fusion | flops 786432 | bytes 2568704 | tf_op jit(solution)/shard_map/scatter-add | solution.py:55
  101.8 0.4 slice_divide_fusion
  102.1 1.6 fusion.25
  103.8 0.0 copy-start.2
  103.8 0.0 all-gather.5.cloned.1.call-update
  103.8 0.0 all-gather.3.cloned.1.call-start
  103.8 0.7 all-gather.3.cloned.1.call-update
  104.5 0.6 copy-done.2
  105.2 0.1 concatenate.14
  105.3 2.3 gather_fusion.1
  107.6 7.5 %all-to-all-start.2 = ((f32[4,64,1536]{2,1,0:T(8,128)}), f32[4,64,1536]{2,1,0:T(8,128)S(1)}, u32[]{:S(2)}, u32[]{:S(2)}) async-start(f32[4,64,1536]{2,1,0:T(8,128)} %bitcast.7), calls=%async_computation.2 | async-start | bytes 3145728 | tf_op jit(solution)/shard_map/all_to_all | solution.py:76
  115.1 67.4 %all-to-all-done.2 = f32[4,64,1536]{2,1,0:T(8,128)S(1)} async-done(((f32[4,64,1536]{2,1,0:T(8,128)}), f32[4,64,1536]{2,1,0:T(8,128)S(1)}, u32[]{:S(2)}, u32[]{:S(2)}) %all-to-all-start.2) | async-done | bytes 1572896 | tf_op jit(solution)/shard_map/all_to_all | solution.py:76
  182.5 3.3 scatter_custom_fusion.4
  185.9 46.1 %all-gather.5.cloned.1.call-done = f32[832,1536]{1,0:T(8,128)} async-done(((f32[208,1536]{1,0:T(8,128)}), f32[832,1536]{1,0:T(8,128)}) %all-gather.5.cloned.1.call-update) | async-done | bytes 5111824 | tf_op jit(solution)/shard_map/all_gather | solution.py:83
  232.0 6.0 %copy.17 = f32[832,1536]{0,1:T(8,128)} copy(f32[832,1536]{1,0:T(8,128)} %all-gather.5.cloned.1.call-done) | data formatting | bytes 10223616 | tf_op jit(solution)/shard_map/all_gather | solution.py:83
  238.0 10.6 %multiply_reduce_fusion = (f32[12,208]{1,0:T(8,128)S(1)}, f32[12,208,832]{2,1,0:T(8,128)S(1)}) fusion(f32[832,12,128]{0,2,1:T(8,128)} %bitcast.53, f32[209,1536]{1,0:T(8,128)S(1)} %scatter_custom_fusion.4, f32[208]{0:T(256)S(1)} %bitcast.64), kind=kOutput, calls=%fused_computation.10 | convolution fusion | flops 3194238464 | bytes 14707456 | tf_op jit(solution)/shard_map/frk,grk->rfg/dot_general | solution.py:88
  248.6 0.0 copy-start
  248.6 3.4 copy-done
  252.0 2.0 fusion
  254.0 74.8 %all-gather.3.cloned.1.call-done = f32[832,1536]{1,0:T(8,128)} async-done(((f32[208,1536]{1,0:T(8,128)}), f32[832,1536]{1,0:T(8,128)}) %all-gather.3.cloned.1.call-update) | async-done | bytes 5111824 | tf_op jit(solution)/shard_map/all_gather | solution.py:84
  328.8 6.1 %copy.16 = f32[832,1536]{0,1:T(8,128)} copy(f32[832,1536]{1,0:T(8,128)} %all-gather.3.cloned.1.call-done) | data formatting | bytes 10223616 | tf_op jit(solution)/shard_map/all_gather | solution.py:84
  334.9 12.9 %divide_bitcast_fusion = f32[12,26,8,128]{3,2,1,0:T(8,128)S(1)} fusion(f32[832,12,128]{0,2,1:T(8,128)} %bitcast.54, f32[12,208,832]{2,1,0:T(8,128)} %copy-done, f32[12,208]{1,0:T(8,128)S(1)} %broadcast_maximum_fusion, f32[208,12]{0,1:T(8,128)S(1)} %bitcast.59), kind=kOutput, calls=%fused_computation.27 | convolution fusion | flops 3194241024 | bytes 14716416 | tf_op jit(solution)/shard_map/tak,ktl->atl/dot_general | solution.py:96
  347.8 0.1 copy.35
  348.0 0.1 concatenate.15
  348.1 2.3 gather_fusion.2
  350.5 6.6 %all-to-all-start.3 = ((f32[4,64,1536]{2,1,0:T(8,128)}), f32[4,64,1536]{2,1,0:T(8,128)S(1)}, u32[]{:S(2)}, u32[]{:S(2)}) async-start(f32[4,64,1536]{2,1,0:T(8,128)} %bitcast.13), calls=%async_computation.3 | async-start | bytes 3145728 | tf_op jit(solution)/shard_map/all_to_all | solution.py:104
  357.1 33.5 %all-to-all-done.3 = f32[4,64,1536]{2,1,0:T(8,128)S(1)} async-done(((f32[4,64,1536]{2,1,0:T(8,128)}), f32[4,64,1536]{2,1,0:T(8,128)S(1)}, u32[]{:S(2)}, u32[]{:S(2)}) %all-to-all-start.3) | async-done | bytes 1572896 | tf_op jit(solution)/shard_map/all_to_all | solution.py:104
  390.6 2.3 gather_fusion.3
  (14 shorter events, 0.1 us)
Async XLA Ops:
  11.0 11.8 %all-to-all-start = ((f32[4,1,64]{2,1,0:T(1,128)}), f32[4,1,64]{2,1,0:T(1,128)S(1)}, u32[]{:S(2)}, u32[]{:S(2)}) async-start(f32[4,1,64]{2,1,0:T(1,128)} %all_to_all.15), calls=%async_computation | async-start | bytes 4096 | tf_op jit(solution)/shard_map/all_to_all | solution.py:69
  22.7 70.7 %all-to-all-start.1 = ((f32[4,64,3072]{2,1,0:T(8,128)}), f32[4,64,3072]{2,1,0:T(8,128)S(1)}, u32[]{:S(2)}, u32[]{:S(2)}) async-start(f32[4,64,3072]{2,1,0:T(8,128)} %bitcast.55), calls=%async_computation.1 | async-start | bytes 6291456 | tf_op jit(solution)/shard_map/all_to_all | solution.py:68
  27.3 204.8 %all-gather.5.cloned.1.call-start = ((), (), s32[]{:S(2)}) async-start(), calls=%async_computation.5 | async-start | bytes 6389760 | tf_op jit(solution)/shard_map/all_gather | solution.py:83
  93.5 1.7 copy-start.1
  103.8 1.4 copy-start.2
  103.8 225.0 %all-gather.3.cloned.1.call-start = ((), (), s32[]{:S(2)}) async-start(), calls=%async_computation.4 | async-start | bytes 6389760 | tf_op jit(solution)/shard_map/all_gather | solution.py:84
  107.6 74.9 %all-to-all-start.2 = ((f32[4,64,1536]{2,1,0:T(8,128)}), f32[4,64,1536]{2,1,0:T(8,128)S(1)}, u32[]{:S(2)}, u32[]{:S(2)}) async-start(f32[4,64,1536]{2,1,0:T(8,128)} %bitcast.7), calls=%async_computation.2 | async-start | bytes 3145728 | tf_op jit(solution)/shard_map/all_to_all | solution.py:76
  248.6 3.4 copy-start
  350.5 40.1 %all-to-all-start.3 = ((f32[4,64,1536]{2,1,0:T(8,128)}), f32[4,64,1536]{2,1,0:T(8,128)S(1)}, u32[]{:S(2)}, u32[]{:S(2)}) async-start(f32[4,64,1536]{2,1,0:T(8,128)} %bitcast.13), calls=%async_computation.3 | async-start | bytes 3145728 | tf_op jit(solution)/shard_map/all_to_all | solution.py:104
Sparse Core Ops, SparseCore 0:
  103.9 128.0 all-gather.4
  233.6 95.1 all-gather.2
where the time goes:
time: 405 us; the launch traced here: 400 us
  waiting for transfers between devices  286 us (71%)
  local copies, waits for them, and re-layouts  33.9 us (8%)
  matrix products  23.5 us (6%)
  starting transfers between devices  23.4 us (6%)
  other arithmetic  19 us (5%)
  between operations  13.5 us (3%)
    all_gather x1, waiting for transfers between devices, local(): portion_values = lax.all_gather(merged_values, 'win', axis=0, tiled=True)  74.8 us
    all_to_all x1, waiting for transfers between devices, local(): lax.all_to_all(packed_queries, 'win', split_axis=0, concat_axis=0, tiled=...  67.4 us
    all_to_all x1, waiting for transfers between devices, local(): lax.all_to_all(packed_pair, 'win', split_axis=0, concat_axis=0, tiled=True)  63.8 us
    all_gather x1, waiting for transfers between devices, local(): portion_keys = lax.all_gather(merged_keys, 'win', axis=0, tiled=True)  46.1 us
    all_to_all x1, waiting for transfers between devices, local(): lax.all_to_all(outgoing, 'win', split_axis=0, concat_axis=0, tiled=True)  33.5 us
    dot_general x1, matrix products, local(): jnp.einsum('tak,ktl->atl', attention_weight, value_head_stack, precision=...  12.9 us
    dot_general x1, matrix products, local(): jnp.einsum('frk,grk->rfg', query_head_stack, key_head_stack, precision=la...  10.6 us
    scatter-add x2, other arithmetic, average_slots(): jax.ops.segment_sum(flattened, segment, MERGED_WINDOW_ROWS + 1)  9.96 us
  transfers between devices with their start and end apart: 6, of which 5 were waited for; matrix products, arithmetic and copies ran while one was open for 8% of the time, Pallas kernels for 0%

commit v1 on v0

v1 whole, which is shorter than its diff:
```python
import functools
import math

import jax
import jax.numpy as jnp
from jax import lax
from jax.experimental import pallas as pl
from jax.experimental.pallas import tpu as pltpu
from jax.sharding import PartitionSpec as P

HEAD_DIM = 128
MERGED_WINDOW_ROWS = 208
SCALING = 1.0 / math.sqrt(HEAD_DIM)
F32 = jnp.float32
BF16 = jnp.bfloat16
MESH = pl.DeviceIdType.MESH


def halves(x):
    high = x.astype(BF16)
    return high, (x - high.astype(F32)).astype(BF16)


def dot(a, b, dims=((1,), (0,))):
    return lax.dot_general(a, b, (dims, ((), ())), preferred_element_type=F32)


def partners_of(me, window_count):
    if window_count == 4:
        return [lax.rem(me + 2, 4), 3 - me, me + 1 - 2 * lax.rem(me, 2)]
    return [lax.rem(me + o, window_count) for o in range(1, window_count)]


def kernel(
    window_count, slots, rows,
    q_ref, k_ref, v_ref, mt_ref, out_ref,
    inbox, outbox, targets, member, same, key_parts, value_parts,
    own_sem, in_send, in_recv, mt_send, mt_recv, out_own, out_send, out_recv,
):
    me = lax.axis_index("win")
    partners = partners_of(me, window_count)
    sources = (q_ref, k_ref, v_ref)
    merged_total = window_count * MERGED_WINDOW_ROWS

    def head_columns(window, slot):
        return pl.ds(pl.multiple_of((window * slots + slot) * HEAD_DIM, HEAD_DIM), HEAD_DIM)

    def own_copy(slot, t):
        return pltpu.make_async_copy(
            sources[t].at[:, head_columns(me, slot)],
            inbox.at[slot, t, pl.ds(pl.multiple_of(me * rows, rows), rows)],
            own_sem.at[slot, t],
        )

    def send_copy(slot, t, to):
        return pltpu.make_async_remote_copy(
            src_ref=sources[t].at[:, head_columns(to, slot)],
            dst_ref=inbox.at[slot, t, pl.ds(pl.multiple_of(me * rows, rows), rows)],
            send_sem=in_send.at[slot, t, to],
            recv_sem=in_recv.at[slot, t, me],
            device_id={"win": to},
            device_id_type=MESH,
        )

    def arrival(slot, t, source):
        return pltpu.make_async_remote_copy(
            src_ref=sources[t].at[:, head_columns(me, slot)],
            dst_ref=inbox.at[slot, t, pl.ds(pl.multiple_of(source * rows, rows), rows)],
            send_sem=in_send.at[slot, t, source],
            recv_sem=in_recv.at[slot, t, source],
            device_id={"win": source},
            device_id_type=MESH,
        )

    def mt_copy(to, slot_of):
        return pltpu.make_async_remote_copy(
            src_ref=mt_ref,
            dst_ref=targets.at[slot_of],
            send_sem=mt_send.at[to],
            recv_sem=mt_recv.at[slot_of],
            device_id={"win": to},
            device_id_type=MESH,
        )

    def return_copy(slot, to):
        return pltpu.make_async_remote_copy(
            src_ref=outbox.at[slot, pl.ds(pl.multiple_of(to * rows, rows), rows)],
            dst_ref=out_ref.at[:, head_columns(me, slot)],
            send_sem=out_send.at[slot, to],
            recv_sem=out_recv.at[slot, me],
            device_id={"win": to},
            device_id_type=MESH,
        )

    def return_arrival(slot, source):
        return pltpu.make_async_remote_copy(
            src_ref=outbox.at[slot, pl.ds(pl.multiple_of(source * rows, rows), rows)],
            dst_ref=out_ref.at[:, head_columns(source, slot)],
            send_sem=out_send.at[slot, source],
            recv_sem=out_recv.at[slot, source],
            device_id={"win": source},
            device_id_type=MESH,
        )

    def return_own(slot):
        return pltpu.make_async_copy(
            outbox.at[slot, pl.ds(pl.multiple_of(me * rows, rows), rows)],
            out_ref.at[:, head_columns(me, slot)],
            out_own.at[slot],
        )

    barrier = pltpu.get_barrier_semaphore()
    for other in partners:
        pl.semaphore_signal(barrier, inc=1, device_id={"win": other}, device_id_type=MESH)
    for slot in range(slots):
        for t in range(3):
            own_copy(slot, t).start()
    pl.semaphore_wait(barrier, window_count - 1)

    for other in partners:
        mt_copy(other, me).start()
    for slot in range(slots):
        for t in (1, 0, 2):
            for other in partners:
                send_copy(slot, t, other).start()

    targets[me] = mt_ref[...]
    for other in partners:
        mt_copy(other, other).wait_recv()
    merged_index = lax.broadcasted_iota(jnp.int32, (merged_total, rows), 0)
    for w in range(window_count):
        member[:, w * rows : (w + 1) * rows] = (
            (merged_index == targets[w]).astype(F32).astype(BF16)
        )
    for w in range(window_count):
        column = jnp.transpose(
            jnp.broadcast_to(targets[w].astype(F32), (HEAD_DIM, rows))
        )[:, :1]
        for u in range(window_count):
            same[w * rows : (w + 1) * rows, u * rows : (u + 1) * rows] = (
                (column == targets[u].astype(F32)).astype(F32).astype(BF16)
            )

    def merge(matrix, source):
        high, low = halves(source)
        total = dot(matrix, high) + dot(matrix, low)
        count = jnp.sum(matrix.astype(F32), axis=1, keepdims=True)
        return total / count

    def one_slot(slot, carry):
        for t in range(3):
            own_copy(slot, t).wait()
            for other in partners:
                arrival(slot, t, other).wait_recv()
        for t, parts in ((1, key_parts), (2, value_parts)):
            high, low = halves(merge(member[...], inbox[slot, t]))
            parts[0] = high
            parts[1] = low

        def one_window(i, carry):
            w = lax.rem(me + 1 + i, window_count)
            chosen = pl.ds(pl.multiple_of(w * rows, rows), rows)
            query = merge(same[chosen], inbox[slot, 0]) * SCALING
            q_high, q_low = halves(query)
            over = ((1,), (1,))
            scores = (
                dot(q_high, key_parts[0], over)
                + dot(q_high, key_parts[1], over)
                + dot(q_low, key_parts[0], over)
            )
            top = jnp.max(scores, axis=1, keepdims=True)
            weight = jnp.exp(scores - top)
            total = jnp.sum(weight, axis=1, keepdims=True)
            w_high, w_low = halves(weight)
            mixed = (
                dot(w_high, value_parts[0])
                + dot(w_high, value_parts[1])
                + dot(w_low, value_parts[0])
            )
            outbox[slot, chosen] = mixed / total

            @pl.when(i < window_count - 1)
            def _():
                return_copy(slot, w).start()

            return carry

        lax.fori_loop(0, window_count, one_window, 0)
        return_own(slot).start()
        return carry

    lax.fori_loop(0, slots, one_slot, 0)

    for other in partners:
        mt_copy(other, me).wait_send()
    for slot in range(slots):
        for t in range(3):
            for other in partners:
                send_copy(slot, t, other).wait_send()
        return_own(slot).wait()
        for other in partners:
            return_copy(slot, other).wait_send()
            return_arrival(slot, other).wait_recv()


def by_heads(queries, key_rows, value_rows, merge_target):
    window_count = lax.axis_size("win")
    rows, col_width = queries.shape
    slots = col_width // HEAD_DIM // window_count
    all_rows = window_count * rows
    merged_total = window_count * MERGED_WINDOW_ROWS
    dma = pltpu.SemaphoreType.DMA
    hbm = pl.BlockSpec(memory_space=pl.ANY)
    flops = 2 * slots * HEAD_DIM * all_rows * (6 * merged_total + 4 * merged_total + 2 * all_rows)
    return pl.pallas_call(
        functools.partial(kernel, window_count, slots, rows),
        out_shape=jax.ShapeDtypeStruct((rows, col_width), F32),
        in_specs=[hbm, hbm, hbm, pl.BlockSpec(memory_space=pltpu.VMEM)],
        out_specs=hbm,
        scratch_shapes=[
            pltpu.VMEM((slots, 3, all_rows, HEAD_DIM), F32),
            pltpu.VMEM((slots, all_rows, HEAD_DIM), F32),
            pltpu.VMEM((window_count, 1, rows), jnp.int32),
            pltpu.VMEM((merged_total, all_rows), BF16),
            pltpu.VMEM((all_rows, all_rows), BF16),
            pltpu.VMEM((2, merged_total, HEAD_DIM), BF16),
            pltpu.VMEM((2, merged_total, HEAD_DIM), BF16),
            dma((slots, 3)),
            dma((slots, 3, window_count)),
            dma((slots, 3, window_count)),
            dma((window_count,)),
            dma((window_count,)),
            dma((slots,)),
            dma((slots, window_count)),
            dma((slots, window_count)),
        ],
        compiler_params=pltpu.CompilerParams(
            collective_id=0, has_side_effects=True, vmem_limit_bytes=48 * 1024 * 1024
        ),
        cost_estimate=pl.CostEstimate(
            flops=flops, bytes_accessed=32 * rows * col_width, transcendentals=0
        ),
    )(queries, key_rows, value_rows, merge_target.reshape(1, rows))


def exact_dot(a, b):
    return jnp.dot(a, b, precision=lax.Precision.HIGHEST)


def by_rows(queries, key_rows, value_rows, merge_target):
    window_count = lax.axis_size("win")
    head_count = queries.shape[1] // HEAD_DIM
    rows = queries.shape[0]
    gathered = [
        lax.all_gather(x, "win", axis=0, tiled=True)
        for x in (queries, key_rows, value_rows, merge_target)
    ]
    all_queries, all_keys, all_values, all_targets = gathered

    def merged_window(window):
        index = window * MERGED_WINDOW_ROWS + jnp.arange(MERGED_WINDOW_ROWS, dtype=jnp.int32)
        member = (index[:, None] == all_targets[None, :]).astype(F32)
        count = jnp.sum(member, axis=1, keepdims=True)
        return exact_dot(member, all_keys) / count, exact_dot(member, all_values) / count

    merged_keys, merged_values = lax.map(merged_window, jnp.arange(window_count, dtype=jnp.int32))
    same = (merge_target[:, None] == all_targets[None, :]).astype(F32)
    own_queries = exact_dot(same, all_queries) / jnp.sum(same, axis=1, keepdims=True)

    def by_head(x):
        return jnp.transpose(x.reshape(-1, head_count, HEAD_DIM), (1, 0, 2))

    def one_head(stack):
        query, key, value = stack
        scores = exact_dot(query, key.T) * SCALING
        weight = jnp.exp(scores - jnp.max(scores, axis=1, keepdims=True))
        return exact_dot(weight, value) / jnp.sum(weight, axis=1, keepdims=True)

    mixed = lax.map(one_head, (by_head(own_queries), by_head(merged_keys), by_head(merged_values)))
    return jnp.transpose(mixed, (1, 0, 2)).reshape(rows, -1)


def local(queries, key_rows, value_rows, merge_target):
    heads = queries.shape[1] // HEAD_DIM
    if heads % lax.axis_size("win") == 0:
        return by_heads(queries, key_rows, value_rows, merge_target)
    return by_rows(queries, key_rows, value_rows, merge_target)


def solution(mesh):
    rows = P(("groups", "win"), ("head", "sub"))
    return jax.shard_map(
        local,
        mesh=mesh,
        in_specs=(rows, rows, rows, P(("groups", "win"))),
        out_specs=rows,
        check_vma=False,
    )
```

time: 405 us -> 145 us (0.36); the launches traced: 400 us -> 144 us
  waiting for transfers between devices: 286 us -> 0 us
  Pallas kernels: 0 us -> 140 us
  local copies, waits for them, and re-layouts: 33.9 us -> 4.64 us
  matrix products: 23.5 us -> 0 us
  starting transfers between devices: 23.4 us -> 0 us
  other arithmetic: 19 us -> 0 us
  between operations: 13.5 us -> 0.01 us
    all_to_all x4 -> x0, waiting for transfers between devices: 165 us -> none  [the longest x1 67.4 us: local(): lax.all_to_all(packed_queries, 'win', split_axis=0, concat_axis=0, tiled=...]
    pallas_call x0 -> x1, Pallas kernels: none -> 140 us  [by_heads(): pl.pallas_call(functools.partial(kernel, window_count, slots, rows), out_...]
    all_gather x2 -> x0, waiting for transfers between devices: 121 us -> none  [the longest x1 74.8 us: local(): portion_values = lax.all_gather(merged_values, 'win', axis=0, tiled=True)]
    dot_general x2 -> x0, matrix products: 23.5 us -> none  [the longest x1 12.9 us: local(): jnp.einsum('tak,ktl->atl', attention_weight, value_head_stack, precision=...]
    all_to_all x4 -> x0, starting transfers between devices: 23.4 us -> none  [the longest x1 7.51 us: local(): lax.all_to_all(packed_queries, 'win', split_axis=0, concat_axis=0, tiled=...]
    scatter-add x3 -> x0, other arithmetic: 12.3 us -> none  [the longest x2 9.96 us: average_slots(): jax.ops.segment_sum(flattened, segment, MERGED_WINDOW_ROWS + 1)]
    all_gather x2 -> x0, local copies, waits for them, and re-layouts: 12.1 us -> none  [the longest x1 6.06 us: local(): portion_values = lax.all_gather(merged_values, 'win', axis=0, tiled=True)]
    gather x4 -> x0, local copies, waits for them, and re-layouts: 10.3 us -> none  [the longest x2 5.67 us: pack_rows(): jnp.concatenate([source, padding], 0)[source_row]]
  transfers between devices with their start and end apart: 6 -> 0, of which waited for: 5 -> 0; matrix products, arithmetic and copies ran while one was open for 8% -> 0% of each run, Pallas kernels for 0% -> 0%
where the time goes in v1:
time: 145 us; the launch traced here: 144 us
  Pallas kernels  140 us (97%)
  local copies, waits for them, and re-layouts  4.64 us (3%)
    pallas_call x1, Pallas kernels, by_heads(): pl.pallas_call(functools.partial(kernel, window_count, slots, rows), out_...  140 us
    unnamed x7, local copies, waits for them, and re-layouts  4.64 us

profile of v1, /device:TPU:9, one launch (start us, length us, event | category | flops | bytes accessed | tf_op | source)
XLA Modules:
  0.0 144.3 jit_solution(7754969025527055966)
XLA Ops:
  0.0 0.0 copy-start
  0.0 1.4 copy-done
  1.4 0.0 copy-start.1
  1.4 1.4 copy-done.1
  2.8 0.0 copy-start.2
  2.8 0.7 copy-done.2
  3.5 139.7 %shard_map.46 = f32[256,1536]{1,0:T(8,128)S(1)} custom-call(f32[256,1536]{1,0:T(8,128)S(1)} %copy-done, f32[256,1536]{1,0:T(8,128)S(1)} %copy-done.1, f32[256,1536]{1,0:T(8,128)} %v_ref.1, s32[1,256]{1,0:T(1,128)S(1)} %bitcast.1), custom_call_target="tpu_custom_call" | custom-call | flops 8153726976 | bytes 12582912 | tf_op jit(solution)/shard_map/pallas_call | solution.py:215
  143.2 1.1 copy.6
Async XLA Ops:
  0.0 1.4 copy-start
  1.4 1.4 copy-start.1
  2.8 0.7 copy-start.2

commit v2 on v1

--- a/solution.py
+++ b/solution.py
@@ -35,7 +35,7 @@
     window_count, slots, rows,
     q_ref, k_ref, v_ref, mt_ref, out_ref,
     inbox, outbox, targets, member, same, key_parts, value_parts,
-    own_sem, in_send, in_recv, mt_send, mt_recv, out_own, out_send, out_recv,
+    mt_own, own_sem, in_send, in_recv, mt_send, mt_recv, out_own, out_send, out_recv,
 ):
     me = lax.axis_index("win")
     partners = partners_of(me, window_count)
@@ -109,9 +109,11 @@
             out_own.at[slot],
         )
 
+    mt_mine = pltpu.make_async_copy(mt_ref, targets.at[me], mt_own)
     barrier = pltpu.get_barrier_semaphore()
     for other in partners:
         pl.semaphore_signal(barrier, inc=1, device_id={"win": other}, device_id_type=MESH)
+    mt_mine.start()
     for slot in range(slots):
         for t in range(3):
             own_copy(slot, t).start()
@@ -124,7 +126,7 @@
             for other in partners:
                 send_copy(slot, t, other).start()
 
-    targets[me] = mt_ref[...]
+    mt_mine.wait()
     for other in partners:
         mt_copy(other, other).wait_recv()
     merged_index = lax.broadcasted_iota(jnp.int32, (merged_total, rows), 0)
@@ -215,7 +217,7 @@
     return pl.pallas_call(
         functools.partial(kernel, window_count, slots, rows),
         out_shape=jax.ShapeDtypeStruct((rows, col_width), F32),
-        in_specs=[hbm, hbm, hbm, pl.BlockSpec(memory_space=pltpu.VMEM)],
+        in_specs=[hbm] * 4,
         out_specs=hbm,
         scratch_shapes=[
             pltpu.VMEM((slots, 3, all_rows, HEAD_DIM), F32),
@@ -225,6 +227,7 @@
             pltpu.VMEM((all_rows, all_rows), BF16),
             pltpu.VMEM((2, merged_total, HEAD_DIM), BF16),
             pltpu.VMEM((2, merged_total, HEAD_DIM), BF16),
+            dma,
             dma((slots, 3)),
             dma((slots, 3, window_count)),
             dma((slots, 3, window_count)),
@@ -235,7 +238,7 @@
             dma((slots, window_count)),
         ],
         compiler_params=pltpu.CompilerParams(
-            collective_id=0, has_side_effects=True, vmem_limit_bytes=48 * 1024 * 1024
+            collective_id=0, has_side_effects=True, vmem_limit_bytes=63 * 1024 * 1024
         ),
         cost_estimate=pl.CostEstimate(
             flops=flops, bytes_accessed=32 * rows * col_width, transcendentals=0

time: 145 us -> 143 us (0.986)
  local copies, waits for them, and re-layouts: 4.64 us -> 2.66 us
    unnamed x7 -> x1, local copies, waits for them, and re-layouts: 4.64 us -> 2.66 us
where the time goes in v2:
time: 143 us
  Pallas kernels  140 us (98%)
  local copies, waits for them, and re-layouts  2.66 us (2%)
    pallas_call x1, Pallas kernels, by_heads(): pl.pallas_call(functools.partial(kernel, window_count, slots, rows), out_...  140 us

profile of v2, /device:TPU:9, one launch (start us, length us, event | category | flops | bytes accessed | tf_op | source)
XLA Modules:
  0.0 142.7 jit_solution(10270464423972343299)
XLA Ops:
  0.0 140.0 %shard_map.46 = f32[256,1536]{1,0:T(8,128)} custom-call(f32[256,1536]{1,0:T(8,128)} %q_ref.1, f32[256,1536]{1,0:T(8,128)} %k_ref.1, f32[256,1536]{1,0:T(8,128)} %v_ref.1, s32[1,256]{1,0:T(1,128)} %bitcast.1), custom_call_target="tpu_custom_call" | custom-call | flops 8153726976 | bytes 12582912 | tf_op jit(solution)/shard_map/pallas_call | solution.py:217
  140.0 2.7 %copy.6 = f32[256,1536]{1,0:T(8,128)} copy(f32[256,1536]{1,0:T(8,128)} %shard_map.46) | data formatting | bytes 3145728

commit v3 on v2

--- a/solution.py
+++ b/solution.py
@@ -216,7 +216,7 @@
     flops = 2 * slots * HEAD_DIM * all_rows * (6 * merged_total + 4 * merged_total + 2 * all_rows)
     return pl.pallas_call(
         functools.partial(kernel, window_count, slots, rows),
-        out_shape=jax.ShapeDtypeStruct((rows, col_width), F32),
+        out_shape=pltpu.VMEM((rows, col_width), F32),
         in_specs=[hbm] * 4,
         out_specs=hbm,
         scratch_shapes=[
@@ -238,7 +238,7 @@
             dma((slots, window_count)),
         ],
         compiler_params=pltpu.CompilerParams(
-            collective_id=0, has_side_effects=True, vmem_limit_bytes=63 * 1024 * 1024
+            collective_id=0, has_side_effects=True, vmem_limit_bytes=60 * 1024 * 1024
         ),
         cost_estimate=pl.CostEstimate(
             flops=flops, bytes_accessed=32 * rows * col_width, transcendentals=0

time: 143 us -> 141 us (0.986)
  local copies, waits for them, and re-layouts: 2.66 us -> 1.15 us
    unnamed x1, local copies, waits for them, and re-layouts: 2.66 us -> 1.15 us
where the time goes in v3:
time: 141 us
  Pallas kernels  140 us (99%)
    pallas_call x1, Pallas kernels, by_heads(): pl.pallas_call(functools.partial(kernel, window_count, slots, rows), out_...  140 us

profile of v3, /device:TPU:9, one launch (start us, length us, event | category | flops | bytes accessed | tf_op | source)
XLA Modules:
  0.0 141.1 jit_solution(16683422956214062808)
XLA Ops:
  0.0 139.9 %shard_map.46 = f32[256,1536]{1,0:T(8,128)S(1)} custom-call(f32[256,1536]{1,0:T(8,128)} %q_ref.1, f32[256,1536]{1,0:T(8,128)} %k_ref.1, f32[256,1536]{1,0:T(8,128)} %v_ref.1, s32[1,256]{1,0:T(1,128)} %bitcast.1), custom_call_target="tpu_custom_call" | custom-call | flops 8153726976 | bytes 12582912 | tf_op jit(solution)/shard_map/pallas_call | solution.py:217
  139.9 1.1 copy.6
